TPU v7x, 32 devices: a whole 2x2x4 slice. The times are simulated.
32 devices in a mesh: row: 8 (over y, x, core), col: 4 (over z).
Axes of the slice: x: 2, y: 2, z: 4, core: 2. Of those that a mesh axis runs over, the one named last changes fastest.
Arguments:
- objects: float32 [2, 2, 1024, 1024], P(None, None, 'row', 'col'), may hold values from -4 to 4
- illumination: float32 [2, 128, 128], replicated, may hold values from -4 to 4
- intensity: float32 [128, 128, 128], P(('row', 'col')), may hold values from 0 to 2
- row_offset: int32 [128], P(('row', 'col')), may hold values from 0 to 127
- col_offset: int32 [128], P(('row', 'col')), may hold values from 0 to 255
Outputs:
- object_grad: float32 [2, 2, 1024, 1024], P(None, None, 'row', 'col')
- probe_grad: float32 [2, 128, 128], replicated
Inputs may be any that keep to these rules, and one draw needn't show every extreme that they name: `row_offset`: the row, within the tile of the device that holds position j, of the window's centre. `col_offset`: the column, within the tile of the device that holds position j, of the window's centre.
All inputs are finite; a program needn't handle non-finite values.
Results may differ from a plain program's by a relative error of at most 0.00013.
Values sent between devices are 32-bit elements; how exact they have to be, the bound alone decides.
No kernel may reach another device: no remote copies, remote signals or barrier semaphores. Data moves between devices by JAX's collectives and lax.ppermute only.
A program may use at most 64 MiB of HBM per device.

v0:
```python
import math

import jax
import jax.numpy as jnp
from jax import lax
from jax.sharding import PartitionSpec as P

highest = lax.Precision.HIGHEST
depth = 0.5


def extended(block, sides, width):
    for axis, dim in sides:
        count = lax.axis_size(axis)
        forward = [(i, i + 1) for i in range(count - 1)]
        backward = [(target, source) for source, target in forward]
        low = lax.ppermute(
            lax.slice_in_dim(block, block.shape[dim] - width, None, axis=dim), axis, forward
        )
        high = lax.ppermute(lax.slice_in_dim(block, 0, width, axis=dim), axis, backward)
        block = jnp.concatenate([low, block, high], axis=dim)
    return block


def fourier_tables(length):
    index = jnp.arange(length, dtype=jnp.int32)
    product_index = index[:, None] * index[None, :] % length
    angle = -2.0 * math.pi / length * product_index.astype(jnp.float32)
    factor = 1.0 / math.sqrt(length)
    return (jnp.cos(angle) * factor, jnp.sin(angle) * factor)


def fresnel_pair(length):
    index = jnp.arange(length, dtype=jnp.int32)
    signed = jnp.where(index < length // 2, index, index - length)
    square = signed[:, None] ** 2 + signed[None, :] ** 2
    angle = -math.pi * depth / length * square.astype(jnp.float32)
    return jnp.stack([jnp.cos(angle), jnp.sin(angle)])


def real_part(values):
    return values[..., 0, :, :]


def imag_part(values):
    return values[..., 1, :, :]


def paired(real_value, imag_value):
    return jnp.stack([real_value, imag_value], axis=-3)


def product(left_field, right_field):
    real_value = real_part(left_field) * real_part(right_field) - imag_part(left_field) * imag_part(
        right_field
    )
    imag_value = real_part(left_field) * imag_part(right_field) + imag_part(left_field) * real_part(
        right_field
    )
    return paired(real_value, imag_value)


def conjugate(values):
    return paired(real_part(values), -imag_part(values))


def spectrum(values, cosine, sine):
    with_cos = jnp.einsum("...jk,kl->...jl", values, cosine, precision=highest)
    with_sin = jnp.einsum("...jk,kl->...jl", values, sine, precision=highest)
    middle = paired(
        real_part(with_cos) - imag_part(with_sin), real_part(with_sin) + imag_part(with_cos)
    )
    with_cos = jnp.einsum("ij,...jk->...ik", cosine, middle, precision=highest)
    with_sin = jnp.einsum("ij,...jk->...ik", sine, middle, precision=highest)
    return paired(
        real_part(with_cos) - imag_part(with_sin), real_part(with_sin) + imag_part(with_cos)
    )


def fold_rows(values, half_size):
    height = values.shape[2]
    edges = jnp.concatenate([values[:, :, :half_size], values[:, :, height - half_size :]], axis=2)
    arrived = extended(edges, (("row", 2),), half_size)
    inside = values[:, :, half_size : height - half_size]
    inside = inside.at[:, :, :half_size].add(arrived[:, :, :half_size])
    return inside.at[:, :, inside.shape[2] - half_size :].add(arrived[:, :, 3 * half_size :])


def fold_cols(values, half_size):
    width = values.shape[3]
    edges = jnp.concatenate(
        [values[:, :, :, :half_size], values[:, :, :, width - half_size :]], axis=3
    )
    arrived = extended(edges, (("col", 3),), half_size)
    inside = values[:, :, :, half_size : width - half_size]
    inside = inside.at[:, :, :, :half_size].add(arrived[:, :, :, :half_size])
    return inside.at[:, :, :, inside.shape[3] - half_size :].add(arrived[:, :, :, 3 * half_size :])


def on_device(objects, illumination, intensity, row_offset, col_offset):
    length = illumination.shape[-1]
    half_size = length // 2
    count = row_offset.shape[0]
    cosine, sine = fourier_tables(length)
    fresnel = fresnel_pair(length)
    anchor = jnp.zeros((), jnp.int32)

    def windows_of(padded):

        def one_window(start_row, start_col):
            return lax.dynamic_slice(padded, (anchor, start_row, start_col), (2, length, length))

        return jax.vmap(one_window)(row_offset, col_offset)

    padded_both = extended(objects, (("row", 2), ("col", 3)), half_size)
    first_window = windows_of(padded_both[0])
    second_window = windows_of(padded_both[1])
    entry = product(illumination, first_window)
    moved = spectrum(product(spectrum(entry, cosine, sine), fresnel), cosine, -sine)
    exit_wave = product(moved, second_window)
    far_field = spectrum(exit_wave, cosine, sine)
    residual = real_part(far_field) ** 2 + imag_part(far_field) ** 2 - intensity
    far_grad = far_field * residual[:, None]
    exit_grad = spectrum(far_grad, cosine, -sine)
    moved_grad = product(conjugate(second_window), exit_grad)
    second_grad = product(conjugate(moved), exit_grad)
    entry_grad = spectrum(
        product(spectrum(moved_grad, cosine, sine), conjugate(fresnel)), cosine, -sine
    )
    first_grad = product(conjugate(illumination), entry_grad)
    probe_local = jnp.sum(product(conjugate(first_window), entry_grad), axis=0)
    stacked = jnp.stack([first_grad, second_grad], axis=1)
    padded_height = objects.shape[2] + 2 * half_size
    padded_width = objects.shape[3] + 2 * half_size

    def place(number, running):
        corner = (anchor, anchor, row_offset[number], col_offset[number])
        previous = lax.dynamic_slice(running, corner, (2, 2, length, length))
        return lax.dynamic_update_slice(running, previous + stacked[number], corner)

    total = lax.fori_loop(
        0, count, place, jnp.zeros((2, 2, padded_height, padded_width), jnp.float32)
    )
    object_grad = fold_cols(fold_rows(total, half_size), half_size)
    probe_total = lax.psum(probe_local, ("row", "col"))
    positions = count * lax.axis_size("row") * lax.axis_size("col")
    return (object_grad, probe_total / math.sqrt(positions))


def solution(mesh):
    return jax.shard_map(
        on_device,
        mesh=mesh,
        in_specs=(
            P(None, None, "row", "col"),
            P(),
            P(("row", "col"), None, None),
            P(("row", "col")),
            P(("row", "col")),
        ),
        out_specs=(P(None, None, "row", "col"), P()),
        check_vma=False,
    )
```

profile of v0, /device:TPU:0, one launch (start us, length us, event | category | flops | bytes accessed | tf_op | source)
XLA Modules:
  0.0 268.6 jit_solution(7176930396643996641)
XLA Ops:
  8.4 2.4 collective-permute-start
  10.7 1.3 collective-permute-start.1
  13.1 3.1 %collective-permute-done.1 = f32[2,2,64,256]{3,2,1,0:T(8,128)S(1)} collective-permute-done((f32[2,2,64,256]{3,2,1,0:T(8,128)S(1)}, f32[2,2,64,256]{3,2,1,0:T(8,128)S(1)}, u32[]{:S(2)}, u32[]{:S(2)}) %collective-permute-start.1) | collective-permute-done | bytes 262176 | tf_op jit(solution)/shard_map/ppermute | solution.py:20
  17.3 3.5 %collective-permute-start.2 = (f32[2,2,256,64]{3,2,1,0:T(8,128)}, f32[2,2,256,64]{3,2,1,0:T(8,128)S(1)}, u32[]{:S(2)}, u32[]{:S(2)}) collective-permute-start(f32[2,2,256,64]{3,2,1,0:T(8,128)} %get-tuple-element.238), channel_id=1, source_target_pairs={{0,1},{1,2},{2,3},{4,5},{5,6},{6,7},{8,9},{9,10},{10,11},{12,13},{... | collective-permute-start | bytes 786440 | tf_op jit(solution)/shard_map/ppermute | solution.py:17
  20.8 1.3 collective-permute-start.3
  23.3 6.2 %collective-permute-done.2 = f32[2,2,256,64]{3,2,1,0:T(8,128)S(1)} collective-permute-done((f32[2,2,256,64]{3,2,1,0:T(8,128)}, f32[2,2,256,64]{3,2,1,0:T(8,128)S(1)}, u32[]{:S(2)}, u32[]{:S(2)}) %collective-permute-start.2) | collective-permute-done | bytes 262176 | tf_op jit(solution)/shard_map/ppermute | solution.py:17
  29.4 4.4 %collective-permute-done.3 = f32[2,2,256,64]{3,2,1,0:T(8,128)S(1)} collective-permute-done((f32[2,2,256,64]{3,2,1,0:T(8,128)S(1)}, f32[2,2,256,64]{3,2,1,0:T(8,128)S(1)}, u32[]{:S(2)}, u32[]{:S(2)}) %collective-permute-start.3) | collective-permute-done | bytes 262176 | tf_op jit(solution)/shard_map/ppermute | solution.py:20
  34.6 8.2 %while.21 = (s32[]{:T(128)}, f32[2,256,384]{2,1,0:T(8,128)S(1)}, s32[4,3]{1,0:T(4,128)S(1)}, f32[4,2,128,128]{3,2,1,0:T(8,128)S(1)}, s32[]{:T(128)}) while((s32[]{:T(128)}, f32[2,256,384]{2,1,0:T(8,128)S(1)}, s32[4,3]{1,0:T(4,128)S(1)}, f32[4,2,128,128]{3,2,1,0:T(8,128)S(1)}, s32[]{:T(128)}) %tuple.113), condition=%wide.while_cond.5, body=%wide.while_body.5.sunk | while | flops 2 | bytes 262261 | solution.py:111
  35.3 1.4 bitcast_dynamic-update-slice_fusion.5
  37.3 1.4 bitcast_dynamic-update-slice_fusion.5
  39.4 1.4 bitcast_dynamic-update-slice_fusion.5
  41.4 1.4 bitcast_dynamic-update-slice_fusion.5
  51.1 8.2 %while.20 = (s32[]{:T(128)}, f32[2,256,384]{2,1,0:T(8,128)S(1)}, s32[4,3]{1,0:T(4,128)S(1)}, f32[4,2,128,128]{3,2,1,0:T(8,128)S(1)}, s32[]{:T(128)}) while((s32[]{:T(128)}, f32[2,256,384]{2,1,0:T(8,128)S(1)}, s32[4,3]{1,0:T(4,128)S(1)}, f32[4,2,128,128]{3,2,1,0:T(8,128)S(1)}, s32[]{:T(128)}) %tuple.121), condition=%wide.while_cond.4, body=%wide.while_body.4.sunk | while | flops 2 | bytes 262261 | solution.py:111
  51.7 1.4 bitcast_dynamic-update-slice_fusion.4
  53.7 1.4 bitcast_dynamic-update-slice_fusion.4
  55.7 1.4 bitcast_dynamic-update-slice_fusion.4
  57.7 1.4 bitcast_dynamic-update-slice_fusion.4
  70.8 1.3 convolution_bitcast_fusion.2
  77.3 33.9 %while.19 = (s32[]{:T(128)}, f32[2,2,256,384]{3,2,1,0:T(8,128)S(1)}, s32[4]{0:T(128)S(1)}, s32[4]{0:T(128)S(1)}, f32[4,2,2,128,128]{4,3,2,0,1:T(8,128)S(1)}, /*index=5*/s32[]{:T(128)}, s32[]{:T(128)}, s32[]{:T(128)}, s32[]{:T(128)}) while((s32[]{:T(128)}, f32[2,2,256,384]{3,2,1,0:T(8,128)S(1)}, s32[4]{0:T(128)S(1)}, s32[4]{0:T(128)S(1)}, ...), condition=%wide.region_1.2_spmd, body=%wide.region_0.1_spmd.sunk | while | flops 65544 | bytes 1310921 | solution.py:141
  82.5 3.3 %dynamic_update_slice.8 = f32[2,2,256,384]{3,2,1,0:T(8,128)S(1)} dynamic-update-slice(f32[2,2,256,384]{3,2,1,0:T(8,128)S(1)} %get-tuple-element.387, f32[2,2,128,128]{3,2,1,0:T(8,128)S(1)} %bitcast_add_fusion.2, s32[]{:T(128)} %constant.166.clone.1..sunk, s32[]{:T(128)} %constant.166.clone.1..sunk, s32[]{:T(128)S(6)} %select_n.206, s32[]{:T(128)S(6)} %select_n.207) | dynamic-update-slice | bytes 524292 | tf_op jit(solution)/shard_map/while/body/eval_jaxpr/dynamic_update_slice | solution.py:139
  91.1 3.1 %dynamic_update_slice.8 = f32[2,2,256,384]{3,2,1,0:T(8,128)S(1)} dynamic-update-slice(f32[2,2,256,384]{3,2,1,0:T(8,128)S(1)} %get-tuple-element.387, f32[2,2,128,128]{3,2,1,0:T(8,128)S(1)} %bitcast_add_fusion.2, s32[]{:T(128)} %constant.166.clone.1..sunk, s32[]{:T(128)} %constant.166.clone.1..sunk, s32[]{:T(128)S(6)} %select_n.206, s32[]{:T(128)S(6)} %select_n.207) | dynamic-update-slice | bytes 524292 | tf_op jit(solution)/shard_map/while/body/eval_jaxpr/dynamic_update_slice | solution.py:139
  99.4 3.1 %dynamic_update_slice.8 = f32[2,2,256,384]{3,2,1,0:T(8,128)S(1)} dynamic-update-slice(f32[2,2,256,384]{3,2,1,0:T(8,128)S(1)} %get-tuple-element.387, f32[2,2,128,128]{3,2,1,0:T(8,128)S(1)} %bitcast_add_fusion.2, s32[]{:T(128)} %constant.166.clone.1..sunk, s32[]{:T(128)} %constant.166.clone.1..sunk, s32[]{:T(128)S(6)} %select_n.206, s32[]{:T(128)S(6)} %select_n.207) | dynamic-update-slice | bytes 524292 | tf_op jit(solution)/shard_map/while/body/eval_jaxpr/dynamic_update_slice | solution.py:139
  107.8 3.4 %dynamic_update_slice.8 = f32[2,2,256,384]{3,2,1,0:T(8,128)S(1)} dynamic-update-slice(f32[2,2,256,384]{3,2,1,0:T(8,128)S(1)} %get-tuple-element.387, f32[2,2,128,128]{3,2,1,0:T(8,128)S(1)} %bitcast_add_fusion.2, s32[]{:T(128)} %constant.166.clone.1..sunk, s32[]{:T(128)} %constant.166.clone.1..sunk, s32[]{:T(128)S(6)} %select_n.206, s32[]{:T(128)S(6)} %select_n.207) | dynamic-update-slice | bytes 524292 | tf_op jit(solution)/shard_map/while/body/eval_jaxpr/dynamic_update_slice | solution.py:139
  112.2 5.9 %collective-permute-start.4 = (f32[2,2,64,384]{3,2,1,0:T(8,128)}, f32[2,2,64,384]{3,2,1,0:T(8,128)}, u32[]{:S(2)}, u32[]{:S(2)}) collective-permute-start(f32[2,2,64,384]{3,2,1,0:T(8,128)} %get-tuple-element.217), channel_id=1, source_target_pairs={{0,4},{4,8},{8,12},{12,16},{16,20},{20,24},{24,28},{1,5},{5,9},{9,... | collective-permute-start | bytes 1179656 | tf_op jit(solution)/shard_map/ppermute | solution.py:17
  118.1 1.3 collective-permute-start.5
  121.2 3.2 %collective-permute-done.5 = f32[2,2,64,384]{3,2,1,0:T(8,128)} collective-permute-done((f32[2,2,64,384]{3,2,1,0:T(8,128)}, f32[2,2,64,384]{3,2,1,0:T(8,128)}, u32[]{:S(2)}, u32[]{:S(2)}) %collective-permute-start.5) | collective-permute-done | bytes 393248 | tf_op jit(solution)/shard_map/ppermute | solution.py:20
  125.6 3.2 %collective-permute-start.6 = (f32[2,2,128,64]{3,2,1,0:T(8,128)S(1)}, f32[2,2,128,64]{3,2,1,0:T(8,128)S(1)}, u32[]{:S(2)}, u32[]{:S(2)}) collective-permute-start(f32[2,2,128,64]{3,2,1,0:T(8,128)S(1)} %get-tuple-element.241), channel_id=1, source_target_pairs={{0,1},{1,2},{2,3},{4,5},{5,6},{6,7},{8,9},{9,10},{10,11},{12,13},{... | collective-permute-start | bytes 393224 | tf_op jit(solution)/shard_map/ppermute | solution.py:17
  128.8 119.8 %all-reduce.2.cloned.1.call-done = f32[2,128,128]{2,1,0:T(8,128)} async-done(((f32[2,128,128]{2,1,0:T(8,128)}), f32[2,128,128]{2,1,0:T(8,128)}) %all-reduce.2.cloned.1.call-update) | async-done | bytes 131088 | tf_op jit(solution)/shard_map/psum | solution.py:145
  248.5 1.6 broadcast_multiply_fusion
  250.3 1.3 collective-permute-start.7
  252.5 7.1 %collective-permute-done.7 = f32[2,2,128,64]{3,2,1,0:T(8,128)S(1)} collective-permute-done((f32[2,2,128,64]{3,2,1,0:T(8,128)S(1)}, f32[2,2,128,64]{3,2,1,0:T(8,128)S(1)}, u32[]{:S(2)}, u32[]{:S(2)}) %collective-permute-start.7) | collective-permute-done | bytes 131104 | tf_op jit(solution)/shard_map/ppermute | solution.py:20
  259.7 1.3 scatter-add.19
  (113 shorter events, 46.0 us)
Async XLA Ops:
  7.2 5.9 %copy-start = (f32[2,2,128,256]{3,2,1,0:T(8,128)S(1)}, f32[2,2,128,256]{3,2,1,0:T(8,128)}, u32[]{:S(2)}) copy-start(f32[2,2,128,256]{3,2,1,0:T(8,128)} %param.15) | copy-start | bytes 1572868
  7.2 241.4 %all-reduce.2.cloned.1.call-start = ((), (), s32[]{:S(2)}) async-start(), calls=%async_computation | async-start | bytes 262144 | tf_op jit(solution)/shard_map/psum | solution.py:145
  8.4 4.7 %collective-permute-start = (f32[2,2,64,256]{3,2,1,0:T(8,128)S(1)}, f32[2,2,64,256]{3,2,1,0:T(8,128)S(1)}, u32[]{:S(2)}, u32[]{:S(2)}) collective-permute-start(f32[2,2,64,256]{3,2,1,0:T(8,128)S(1)} %get-tuple-element.249), channel_id=1, source_target_pairs={{0,4},{4,8},{8,12},{12,16},{16,20},{20,24},{24,28},{1,5},{5,9},{9,... | collective-permute-start | bytes 786440 | tf_op jit(solution)/shard_map/ppermute | solution.py:17
  10.7 5.5 %collective-permute-start.1 = (f32[2,2,64,256]{3,2,1,0:T(8,128)S(1)}, f32[2,2,64,256]{3,2,1,0:T(8,128)S(1)}, u32[]{:S(2)}, u32[]{:S(2)}) collective-permute-start(f32[2,2,64,256]{3,2,1,0:T(8,128)S(1)} %get-tuple-element.248), channel_id=1, source_target_pairs={{4,0},{8,4},{12,8},{16,12},{20,16},{24,20},{28,24},{5,1},{9,5},{13... | collective-permute-start | bytes 786440 | tf_op jit(solution)/shard_map/ppermute | solution.py:20
  13.1 9.1 %copy-start.2 = (f32[4,128,128]{2,1,0:T(8,128)S(1)}, f32[4,128,128]{2,1,0:T(8,128)}, u32[]{:S(2)}) copy-start(f32[4,128,128]{2,1,0:T(8,128)} %param.17) | copy-start | bytes 786436
  17.3 12.2 %collective-permute-start.2 = (f32[2,2,256,64]{3,2,1,0:T(8,128)}, f32[2,2,256,64]{3,2,1,0:T(8,128)S(1)}, u32[]{:S(2)}, u32[]{:S(2)}) collective-permute-start(f32[2,2,256,64]{3,2,1,0:T(8,128)} %get-tuple-element.238), channel_id=1, source_target_pairs={{0,1},{1,2},{2,3},{4,5},{5,6},{6,7},{8,9},{9,10},{10,11},{12,13},{... | collective-permute-start | bytes 786440 | tf_op jit(solution)/shard_map/ppermute | solution.py:17
  20.8 13.1 %collective-permute-start.3 = (f32[2,2,256,64]{3,2,1,0:T(8,128)S(1)}, f32[2,2,256,64]{3,2,1,0:T(8,128)S(1)}, u32[]{:S(2)}, u32[]{:S(2)}) collective-permute-start(f32[2,2,256,64]{3,2,1,0:T(8,128)S(1)} %get-tuple-element.239), channel_id=1, source_target_pairs={{1,0},{2,1},{3,2},{5,4},{6,5},{7,6},{9,8},{10,9},{11,10},{13,12},{... | collective-permute-start | bytes 786440 | tf_op jit(solution)/shard_map/ppermute | solution.py:20
  76.6 0.7 copy-start.3
  76.6 0.7 copy-start.4
  112.2 8.0 %collective-permute-start.4 = (f32[2,2,64,384]{3,2,1,0:T(8,128)}, f32[2,2,64,384]{3,2,1,0:T(8,128)}, u32[]{:S(2)}, u32[]{:S(2)}) collective-permute-start(f32[2,2,64,384]{3,2,1,0:T(8,128)} %get-tuple-element.217), channel_id=1, source_target_pairs={{0,4},{4,8},{8,12},{12,16},{16,20},{20,24},{24,28},{1,5},{5,9},{9,... | collective-permute-start | bytes 1179656 | tf_op jit(solution)/shard_map/ppermute | solution.py:17
  118.1 6.3 %collective-permute-start.5 = (f32[2,2,64,384]{3,2,1,0:T(8,128)}, f32[2,2,64,384]{3,2,1,0:T(8,128)}, u32[]{:S(2)}, u32[]{:S(2)}) collective-permute-start(f32[2,2,64,384]{3,2,1,0:T(8,128)} %get-tuple-element.216), channel_id=1, source_target_pairs={{4,0},{8,4},{12,8},{16,12},{20,16},{24,20},{28,24},{5,1},{9,5},{13... | collective-permute-start | bytes 1179656 | tf_op jit(solution)/shard_map/ppermute | solution.py:20
  125.6 126.0 %collective-permute-start.6 = (f32[2,2,128,64]{3,2,1,0:T(8,128)S(1)}, f32[2,2,128,64]{3,2,1,0:T(8,128)S(1)}, u32[]{:S(2)}, u32[]{:S(2)}) collective-permute-start(f32[2,2,128,64]{3,2,1,0:T(8,128)S(1)} %get-tuple-element.241), channel_id=1, source_target_pairs={{0,1},{1,2},{2,3},{4,5},{5,6},{6,7},{8,9},{9,10},{10,11},{12,13},{... | collective-permute-start | bytes 393224 | tf_op jit(solution)/shard_map/ppermute | solution.py:17
  250.3 9.2 %collective-permute-start.7 = (f32[2,2,128,64]{3,2,1,0:T(8,128)S(1)}, f32[2,2,128,64]{3,2,1,0:T(8,128)S(1)}, u32[]{:S(2)}, u32[]{:S(2)}) collective-permute-start(f32[2,2,128,64]{3,2,1,0:T(8,128)S(1)} %get-tuple-element.240), channel_id=1, source_target_pairs={{1,0},{2,1},{3,2},{5,4},{6,5},{7,6},{9,8},{10,9},{11,10},{13,12},{... | collective-permute-start | bytes 393224 | tf_op jit(solution)/shard_map/ppermute | solution.py:20
  260.9 0.8 copy-start.1
Sparse Core Ops, SparseCore 0:
  120.2 128.2 all-reduce.1
where the time goes:
time: 269 us
  waiting for transfers between devices  144 us (54%)
  local copies, waits for them, and re-layouts  40.9 us (15%)
  matrix products  24 us (9%)
  starting transfers between devices  20.1 us (7%)
  loops' own time  16.1 us (6%)
  between operations  14.6 us (5%)
  other arithmetic  9.12 us (3%)
    psum x1, waiting for transfers between devices, on_device(): probe_total = lax.psum(probe_local, ('row', 'col'))  120 us
    ppermute x4, waiting for transfers between devices, extended(): lax.ppermute(lax.slice_in_dim(block, 0, width, axis=dim), axis, backward)  17.8 us
    gather x24, local copies, waits for them, and re-layouts  16 us
    another operation x1, loops' own time, on_device(): lax.fori_loop(0, count, place, jnp.zeros((2, 2, padded_height, padded_wid...  15.7 us
    ppermute x4, starting transfers between devices, extended(): lax.ppermute(lax.slice_in_dim(block, block.shape[dim] - width, None, axis...  14.9 us
    dynamic_update_slice x4, local copies, waits for them, and re-layouts, place(): return lax.dynamic_update_slice(running, previous + stacked[number], corner)  13 us
    dot_general x6, matrix products, spectrum(): with_sin = jnp.einsum('ij,...jk->...ik', sine, middle, precision=highest)  6.24 us
    ppermute x4, waiting for transfers between devices, extended(): lax.ppermute(lax.slice_in_dim(block, block.shape[dim] - width, None, axis...  6.17 us
  transfers between devices with their start and end apart: 9, of which 6 were waited for; matrix products, arithmetic and copies ran while one was open for 3% of the time, Pallas kernels for 0%

commit v1 on v0

v1 whole, which is shorter than its diff:
```python
import functools
import math

import jax
import jax.numpy as jnp
import ml_dtypes
import numpy as np
from jax import lax
from jax.experimental import pallas as pl
from jax.experimental.pallas import tpu as pltpu
from jax.sharding import PartitionSpec as P

depth = 0.5
LANES = 128
GROUP = 2


def split_host(values):
    high = values.astype(ml_dtypes.bfloat16)
    low = (values - high.astype(np.float64)).astype(ml_dtypes.bfloat16)
    return high, low


def operator_tables(length):
    index = np.arange(length)
    angle = -2.0 * math.pi / length * (index[:, None] * index[None, :] % length)
    fourier = np.exp(1j * angle) / math.sqrt(length)
    signed = np.where(index < length // 2, index, index - length)
    phase = np.exp(-1j * math.pi * depth / length * signed.astype(np.float64) ** 2)
    spread = np.conj(fourier) @ (phase[:, None] * fourier)
    spread = 0.5 * (spread + spread.T)
    tables = []
    for operator in (fourier, spread):
        real, imag = operator.real, operator.imag
        right = np.block([[real, imag], [-imag, real]])
        left = np.block([[real, -imag], [imag, real]])
        for block in (right, left):
            tables.extend(split_host(block))
    return np.stack(tables)


def split(values):
    high = values.astype(jnp.bfloat16)
    low = (values - high.astype(jnp.float32)).astype(jnp.bfloat16)
    return high, low


def dot(left, right):
    return jnp.dot(left, right, preferred_element_type=jnp.float32)


def halves(parity, length):
    near = pl.ds(pl.multiple_of(parity * length, length), length)
    far = pl.ds(pl.multiple_of((1 - parity) * length, length), length)
    return near, far


def side_strips(first, last, half):
    lane = lax.broadcasted_iota(jnp.int32, first[0].shape, 1)
    left = jnp.where(lane < half, first[0], pltpu.roll(first[1], half, 1))
    right = jnp.where(lane >= half, last[0], pltpu.roll(last[1], half, 1))
    return left, right


def kept(place, values):
    return jnp.where(place[0] >= 2, values, 0.0)


def pack_kernel(row_place, col_place, objects, row_cross, row_mate, col_cross, col_mate):
    half = row_cross.shape[1]
    outward, inward = halves(lax.rem(row_place[0], 2), half)
    even = lax.rem(col_place[0], 2) == 0
    for part in range(2):
        for comp in range(2):
            for tile in range(2):
                cols = slice(tile * LANES, (tile + 1) * LANES)
                row_cross[4 * part + 2 * comp + tile] = kept(
                    row_place, objects[part, comp, outward, cols]
                )
                row_mate[4 * part + 2 * comp + tile] = objects[part, comp, inward, cols]
        left, right = side_strips(
            (objects[part, 0, :, :LANES], objects[part, 1, :, :LANES]),
            (objects[part, 0, :, LANES:], objects[part, 1, :, LANES:]),
            half,
        )
        col_cross[part] = kept(col_place, jnp.where(even, left, right))
        col_mate[part] = jnp.where(even, right, left)


def corner_kernel(col_place, rows, ahead, col_mate, col_cross):
    half = rows.shape[1]
    even = lax.rem(col_place[0], 2) == 0
    for part in range(2):
        left, right = side_strips(
            (rows[4 * part], rows[4 * part + 2]),
            (rows[4 * part + 1], rows[4 * part + 3]),
            half,
        )
        col_cross[part] = kept(col_place, jnp.where(even, left, right))
        col_mate[part] = jnp.where(even, right, left)


def place_of(offsets, number):
    count = offsets.shape[0] // 2
    row = jnp.max(offsets[number : number + 1, :]).astype(jnp.int32)
    start = jnp.max(offsets[count + number : count + number + 1, :]).astype(jnp.int32)
    return row, start // LANES, lax.rem(start, LANES)


def outer_rows(row_place, beyond):
    half = LANES // 2
    outside = pl.ds(pl.multiple_of(row_place * beyond, half), half)
    inside = pl.ds(pl.multiple_of((1 - row_place) * beyond, half), half)
    return outside, inside


def turned(values, comp):
    return values if comp == 0 else pltpu.roll(values, LANES // 2, 1)


def prepare_kernel(
    row_far, col_far, objects_far, tables_far, probe_far, intensity_far,
    padded, tables, probe, intensity, offsets, row_offset, col_offset, arrived,
):
    half = LANES // 2
    height = objects_far.shape[2]
    pairs = [(row_far, row_offset), (col_far, col_offset)]
    for part in range(2):
        for comp in range(2):
            for tile in range(2):
                cols = slice(tile * LANES, (tile + 1) * LANES)
                pairs.append(
                    (
                        objects_far.at[part, comp, :, cols],
                        padded.at[2 * part + comp, 1 + tile, half : half + height],
                    )
                )
    pairs += [(tables_far, tables), (probe_far, probe), (intensity_far, intensity)]
    copies = [
        pltpu.make_async_copy(source, target, arrived.at[number])
        for number, (source, target) in enumerate(pairs)
    ]
    for copy in copies:
        copy.start()
    for copy in copies:
        copy.wait()
    count = offsets.shape[0] // 2
    for number in range(count):
        row = row_offset[number].astype(jnp.float32)
        start = (col_offset[number] + half).astype(jnp.float32)
        offsets[number] = jnp.full((LANES,), row, jnp.float32)
        offsets[count + number] = jnp.full((LANES,), start, jnp.float32)


def frame_kernel(
    row_place, col_place, row_cross, row_mate, col_mate, col_cross, padded_in, padded, *inner
):
    half = LANES // 2
    _, inward = halves(lax.rem(row_place[0], 2), half)
    near = jnp.concatenate(
        [strip[part, inward] for strip in (col_cross, col_mate) for part in range(2)]
    )
    start = 0
    for piece in inner:
        piece[...] = near[start : start + piece.shape[0]]
        start += piece.shape[0]
    height = col_mate.shape[1]
    outside, inside = outer_rows(lax.rem(row_place[0], 2), half + height)
    cross_tile = 3 * lax.rem(col_place[0], 2)
    mate_tile = 3 - cross_tile
    for part in range(2):
        for comp in range(2):
            ch = 2 * part + comp
            for tile in range(2):
                padded[ch, 1 + tile, outside] = row_cross[2 * ch + tile]
                padded[ch, 1 + tile, inside] = row_mate[2 * ch + tile]
            for tile, strip in ((cross_tile, col_cross), (mate_tile, col_mate)):
                padded[ch, tile, half : half + height] = turned(strip[part], comp)


def main_kernel(
    scale, row_place, col_place, tables, probe, intensity, offsets,
    corner_mate, corner_cross, inner_0, inner_1, inner_2, padded_in,
    padded, own, edge_cross, strip_cross, mate, side_cross, side_mate,
    probe_keep, probe_send, total,
):
    half = LANES // 2
    count = intensity.shape[0]
    lane = lax.broadcasted_iota(jnp.int32, (LANES, LANES), 1)
    outside, inside = outer_rows(lax.rem(row_place[0], 2), padded.shape[2] - half)
    cross_tile = 3 * lax.rem(col_place[0], 2)
    mate_tile = 3 - cross_tile
    inner = jnp.concatenate([inner_0[...], inner_1[...], inner_2[...]])
    for part in range(2):
        for comp in range(2):
            ch = 2 * part + comp
            for side, tile, corner in (
                (0, cross_tile, corner_cross),
                (1, mate_tile, corner_mate),
            ):
                padded[ch, tile, outside] = turned(corner[part], comp)
                at = (2 * side + part) * half
                padded[ch, tile, inside] = turned(inner[at : at + half], comp)
    places = [place_of(offsets, number) for number in range(count)]

    def window(number, ch):
        row, tile, shift = places[number]
        back = lax.rem(LANES - shift, LANES)
        first = pltpu.roll(padded[ch, tile, pl.ds(row, LANES), :], back, 1)
        second = pltpu.roll(padded[ch, tile + 1, pl.ds(row, LANES), :], back, 1)
        return jnp.where(lane < LANES - shift, first, second)

    def from_right(pairs, operator, conjugated):
        at = 4 * operator + (2 if conjugated else 0)
        entry = jnp.concatenate([jnp.concatenate(pair, axis=1) for pair in pairs], axis=0)
        high, low = split(entry)
        return dot(
            jnp.concatenate([high, low, high], axis=1),
            jnp.concatenate([tables[at], tables[at], tables[at + 1]], axis=0),
        )

    def from_left(middle, operator, conjugated):
        at = 4 * operator + (0 if conjugated else 2)
        members = middle.shape[0] // LANES
        stacked = jnp.concatenate(
            [
                jnp.concatenate(
                    [
                        middle[j * LANES : (j + 1) * LANES, c * LANES : (c + 1) * LANES]
                        for j in range(members)
                    ],
                    axis=1,
                )
                for c in range(2)
            ],
            axis=0,
        )
        high, low = split(stacked)
        final = dot(
            jnp.concatenate([tables[at], tables[at], tables[at + 1]], axis=1),
            jnp.concatenate([high, low, high], axis=0),
        )
        return [
            (
                final[:LANES, j * LANES : (j + 1) * LANES],
                final[LANES:, j * LANES : (j + 1) * LANES],
            )
            for j in range(members)
        ]

    def transform(groups, operator, conjugated):
        middles = [from_right(pairs, operator, conjugated) for pairs in groups]
        return [from_left(middle, operator, conjugated) for middle in middles]

    def times(left, right):
        return (left[0] * right[0] - left[1] * right[1], left[0] * right[1] + left[1] * right[0])

    def conj_times(left, right):
        return (left[0] * right[0] + left[1] * right[1], left[0] * right[1] - left[1] * right[0])

    illumination = (probe[0], probe[1])
    numbers = [
        list(range(first, min(first + GROUP, count))) for first in range(0, count, GROUP)
    ]
    w1 = [[(window(j, 0), window(j, 1)) for j in group] for group in numbers]
    moved = transform([[times(illumination, w) for w in group] for group in w1], 1, False)
    w2 = [[(window(j, 2), window(j, 3)) for j in group] for group in numbers]
    far = transform(
        [[times(b, w) for b, w in zip(*group)] for group in zip(moved, w2)], 0, False
    )
    far_grad = []
    for group, values in zip(numbers, far):
        far_grad.append([])
        for j, psi in zip(group, values):
            residual = psi[0] * psi[0] + psi[1] * psi[1] - intensity[j]
            far_grad[-1].append((residual * psi[0], residual * psi[1]))
    exit_grad = transform(far_grad, 0, True)
    moved_grad = [[conj_times(w, g) for w, g in zip(*group)] for group in zip(w2, exit_grad)]
    total[...] = jnp.zeros_like(total)

    def add(number, ch, values):
        row, tile, shift = places[number]
        rows = pl.ds(row, LANES)
        rolled = pltpu.roll(values, shift, 1)
        total[ch, tile, rows, :] += jnp.where(lane >= shift, rolled, 0.0)
        total[ch, tile + 1, rows, :] += jnp.where(lane < shift, rolled, 0.0)

    for group, waves, grads in zip(numbers, moved, exit_grad):
        for j, b, g in zip(group, waves, grads):
            second = conj_times(b, g)
            add(j, 2, second[0])
            add(j, 3, second[1])
    entry_grad = transform(moved_grad, 1, True)
    sums = None
    for windows, grads in zip(w1, entry_grad):
        for w, g in zip(windows, grads):
            term = conj_times(w, g)
            sums = term if sums is None else (sums[0] + term[0], sums[1] + term[1])
    upper = lax.rem(row_place[0], 2) == 0
    probe_keep[...] = scale * jnp.where(upper, sums[0], sums[1])
    probe_send[...] = scale * jnp.where(upper, sums[1], sums[0])
    for group, grads in zip(numbers, entry_grad):
        for j, g in zip(group, grads):
            first = conj_times(illumination, g)
            add(j, 0, first[0])
            add(j, 1, first[1])

    height = own.shape[2]
    even = lax.rem(col_place[0], 2) == 0
    for part in range(2):
        real, imag = 2 * part, 2 * part + 1
        for comp in range(2):
            ch = 2 * part + comp
            for tile in range(2):
                cols = slice(tile * LANES, (tile + 1) * LANES)
                own[part, comp, :, cols] = total[ch, 1 + tile, half : half + height]
                edge_cross[2 * ch + tile] = kept(row_place, total[ch, 1 + tile, outside])
                mate[2 * ch + tile] = total[ch, 1 + tile, inside]
        for rows, cross_at, mate_at in (
            (slice(half, half + height), (side_cross, part), (side_mate, part)),
            (outside, (strip_cross, part), (strip_cross, 2 + part)),
            (inside, (mate, 8 + part), (mate, 10 + part)),
        ):
            right, left = side_strips(
                (total[real, 3, rows], total[imag, 3, rows]),
                (total[real, 0, rows], total[imag, 0, rows]),
                half,
            )
            if rows is outside:
                left, right = kept(row_place, left), kept(row_place, right)
            cross_at[0][cross_at[1]] = jnp.where(even, left, right)
            mate_at[0][mate_at[1]] = jnp.where(even, right, left)


def sides_kernel(
    row_place, col_place, side_cross, side_mate, row_cross, row_mate, out_cross, out_mate
):
    near, far = halves(lax.rem(row_place[0], 2), row_cross.shape[1])
    for part in range(2):
        for rows, source, at in ((near, row_cross, part), (far, row_mate, 8 + part)):
            out_cross[part, rows] = kept(col_place, side_cross[part, rows] + source[at])
            out_mate[part, rows] = side_mate[part, rows] + source[at + 2]


def fold_kernel(
    row_place, col_place, own, row_cross, row_mate, col_mate, col_cross, out
):
    half = row_cross.shape[1]
    near, far = halves(lax.rem(row_place[0], 2), half)
    even = lax.rem(col_place[0], 2) == 0
    lane = lax.broadcasted_iota(jnp.int32, (half, LANES), 1)
    for part in range(2):
        for rows, source in ((near, row_cross), (far, row_mate)):
            cross = col_cross[part, rows]
            mate = col_mate[part, rows]
            left = jnp.where(even, cross, mate)
            right = jnp.where(even, mate, cross)
            for comp in range(2):
                ch = 2 * part + comp

                for tile in range(2):
                    cols = slice(tile * LANES, (tile + 1) * LANES)
                    if tile == 0:
                        side = jnp.where(lane < half, turned(left, comp), 0.0)
                    else:
                        side = jnp.where(lane >= half, turned(right, comp), 0.0)
                    out[part, comp, rows, cols] = (
                        own[part, comp, rows, cols] + side + source[2 * ch + tile]
                    )


def join_kernel(row_place, probe_half, probe_other, out):
    parity = lax.rem(row_place[0], 2)
    out[parity] = probe_half[...]
    out[1 - parity] = probe_other[...]


def add_kernel(left, right, out):
    out[...] = left[...] + right[...]


def local_call(
    kernel, out_shape, inputs, scalars=0, far=(), out_far=(), where=(), scratch=(),
    aliases=None, flops=0, size=1 << 20, vmem=6,
):
    near = pl.BlockSpec(memory_space=pltpu.VMEM)
    places = [
        pl.BlockSpec(memory_space=pltpu.SMEM)
        if number < scalars
        else pl.BlockSpec(memory_space=pltpu.HBM)
        if number in far
        else pl.BlockSpec(memory_space=pl.ANY)
        if number in where
        else near
        for number in range(len(inputs))
    ]
    shapes = [
        shape
        if isinstance(shape, jax.ShapeDtypeStruct)
        else jax.ShapeDtypeStruct(shape, jnp.float32)
        for shape in out_shape
    ]
    return pl.pallas_call(
        kernel,
        out_shape=shapes,
        in_specs=places,
        out_specs=[
            pl.BlockSpec(memory_space=pltpu.HBM) if number in out_far else near
            for number in range(len(out_shape))
        ],
        scratch_shapes=list(scratch),
        input_output_aliases=aliases or {},
        cost_estimate=pl.CostEstimate(flops=flops, bytes_accessed=size, transcendentals=0),
        compiler_params=pltpu.CompilerParams(vmem_limit_bytes=vmem << 20),
    )(*(
        pltpu.with_memory_space_constraint(value, pltpu.HBM) if number in far else value
        for number, value in enumerate(inputs)
    ))


def swap(values, axis, first, wrap=False):
    count = lax.axis_size(axis)
    partner = list(range(count))
    for i in range(first, count - 1, 2):
        partner[i], partner[i + 1] = i + 1, i
    if wrap:
        partner[0], partner[-1] = count - 1, 0
    return lax.ppermute(values, axis, list(enumerate(partner)))


def swap_inner_cols(values):
    rows, cols = lax.axis_size("row"), lax.axis_size("col")
    pairs = []
    for row in range(rows):
        for col in range(cols):
            to_row, to_col = row, col - 1 + 2 * (col % 2)
            if to_col < 0 or to_col >= cols:
                to_row, to_col = row + 1 - 2 * (row % 2), col
            pairs.append((row * cols + col, to_row * cols + to_col))
    return lax.ppermute(values, ("row", "col"), pairs)


def doubled(values, axis, bit):
    pairs = [(i, i ^ bit) for i in range(lax.axis_size(axis))]
    return added(values, lax.ppermute(values, axis, pairs))


def added(left, right):
    return local_call(add_kernel, [left.shape], [left, right])[0]


def on_device(objects, illumination, intensity, row_offset, col_offset):
    length = illumination.shape[-1]
    half = length // 2
    count = row_offset.shape[0]
    height, width = objects.shape[2:]
    tables = jnp.asarray(operator_tables(length))
    axes = ("row", "col")
    positions = count * lax.axis_size("row") * lax.axis_size("col")
    place = []
    for axis in axes:
        spot = lax.axis_index(axis).astype(jnp.int32)
        beyond = spot - 1 + 2 * lax.rem(spot, 2)
        inner = jnp.where((beyond >= 0) & (beyond < lax.axis_size(axis)), 2, 0)
        place.append((lax.rem(spot, 2) + inner).astype(jnp.int32).reshape(1))

    strip = (2, height, LANES)
    band = (8, half, LANES)
    corner = (4, half, LANES)
    field = (4, 4, height + 2 * half, LANES)
    row_cross, row_mate, col_cross, col_mate = local_call(
        pack_kernel,
        [band, band, strip, strip],
        [*place, objects],
        scalars=2,
    )
    row_cross = swap(row_cross, "row", 1, True)
    col_mate = swap(col_mate, "col", 0)
    col_cross = swap_inner_cols(col_cross)
    row_mate = swap(row_mate, "row", 0)
    padded, tables, probe, intensity, offsets = local_call(
        prepare_kernel,
        [
            field, jax.ShapeDtypeStruct(tables.shape, tables.dtype),
            illumination.shape, intensity.shape, (2 * count, LANES),
        ],
        [row_offset, col_offset, objects, tables, illumination, intensity],
        far=(0, 1, 2, 3, 4, 5),
        scratch=[
            pltpu.SMEM(row_offset.shape, jnp.int32),
            pltpu.SMEM(col_offset.shape, jnp.int32),
            pltpu.SemaphoreType.DMA((13,)),
        ],
        size=4 << 20,
        vmem=10,
    )
    corner_mate, corner_cross = local_call(
        corner_kernel,
        [(2, half, LANES), (2, half, LANES)],
        [place[1], row_cross, offsets],
        scalars=1,
        where=(2,),
    )
    corner_mate = swap(corner_mate, "col", 0)
    corner_cross = swap_inner_cols(corner_cross)
    third = -(-4 * half // 24) * 8
    padded, *inner = local_call(
        frame_kernel,
        [field, (third, LANES), (third, LANES), (4 * half - 2 * third, LANES)],
        [*place, row_cross, row_mate, col_mate, col_cross, padded],
        scalars=2,
        aliases={6: 0},
        vmem=10,
    )
    inner = [swap(piece, "row", 0) for piece in inner]
    (
        _, own, edge_cross, strip_cross, mate, side_cross, side_mate, probe_keep, probe_send,
    ) = local_call(
        functools.partial(main_kernel, 1.0 / math.sqrt(positions)),
        [
            field, objects.shape, band, corner, (12, half, LANES), strip, strip,
            (length, length), (length, length),
        ],
        [
            *place, tables, probe, intensity, offsets, corner_mate, corner_cross, *inner, padded,
        ],
        scalars=2,
        scratch=[pltpu.VMEM(field, jnp.float32)],
        aliases={11: 0},
        flops=3 * 2 * 256**3 * 16,
        size=8 << 20,
        vmem=18,
    )
    probe_half = added(probe_keep, swap(probe_send, "row", 0))
    for axis, bit in (("row", 2), ("col", 1)):
        while bit < lax.axis_size(axis):
            probe_half = doubled(probe_half, axis, bit)
            bit *= 2
    probe_other = swap(probe_half, "row", 0)
    strip_cross = swap(strip_cross, "row", 1, True)
    mate = swap(mate, "row", 0)
    edge_cross = swap(edge_cross, "row", 1, True)
    side_cross, side_mate = local_call(
        sides_kernel,
        [strip, strip],
        [*place, side_cross, side_mate, strip_cross, mate],
        scalars=2,
    )
    side_mate = swap(side_mate, "col", 0)
    side_cross = swap_inner_cols(side_cross)
    (object_grad,) = local_call(
        fold_kernel,
        [objects.shape],
        [*place, own, edge_cross, mate, side_mate, side_cross],
        scalars=2,
    )
    (probe_grad,) = local_call(
        join_kernel, [illumination.shape], [place[0], probe_half, probe_other], scalars=1
    )
    return (object_grad, probe_grad)


def solution(mesh):
    return jax.shard_map(
        on_device,
        mesh=mesh,
        in_specs=(
            P(None, None, "row", "col"),
            P(),
            P(("row", "col"), None, None),
            P(("row", "col")),
            P(("row", "col")),
        ),
        out_specs=(P(None, None, "row", "col"), P()),
        check_vma=False,
    )
```

time: 269 us -> 47.1 us (0.18)
  waiting for transfers between devices: 144 us -> 15.1 us
  local copies, waits for them, and re-layouts: 40.9 us -> 1.04 us
  matrix products: 24 us -> 0 us
  loops' own time: 16.1 us -> 0 us
  between operations: 14.6 us -> 0.77 us
  other arithmetic: 9.12 us -> 0 us
  Pallas kernels: 0 us -> 7.58 us
    psum x1 -> x0, waiting for transfers between devices: 120 us -> none  [on_device(): probe_total = lax.psum(probe_local, ('row', 'col'))]
    dot_general x24 -> x0, matrix products: 24 us -> none  [the longest x6 6.24 us: spectrum(): with_sin = jnp.einsum('ij,...jk->...ik', sine, middle, precision=highest)]
    another operation x3 -> x0, loops' own time: 16.1 us -> none  [the longest x1 15.7 us: on_device(): lax.fori_loop(0, count, place, jnp.zeros((2, 2, padded_height, padded_wid...]
    gather x24 -> x0, local copies, waits for them, and re-layouts: 16 us -> none
    dynamic_update_slice x4 -> x0, local copies, waits for them, and re-layouts: 13 us -> none  [place(): return lax.dynamic_update_slice(running, previous + stacked[number], corner)]
    ppermute x8 -> x20, waiting for transfers between devices: 23.9 us -> 15.1 us  [the longest x4 8.85 us: doubled(): return added(values, lax.ppermute(values, axis, pairs))]
    pallas_call x0 -> x13, Pallas kernels: none -> 7.58 us  [local_call(): pl.pallas_call(kernel, out_shape=shapes, in_specs=places, out_specs=[pl.B...]
    dynamic_slice x8 -> x0, local copies, waits for them, and re-layouts: 4.7 us -> none  [place(): corner = (anchor, anchor, row_offset[number], col_offset[number])]
  transfers between devices with their start and end apart: 9 -> 20, of which waited for: 6 -> 10; matrix products, arithmetic and copies ran while one was open for 3% -> 0% of each run, Pallas kernels for 0% -> 6%
where the time goes in v1:
time: 47.1 us; the launch traced here: 46.9 us
  starting transfers between devices  22.5 us (48%)
  waiting for transfers between devices  15.1 us (32%)
  Pallas kernels  7.58 us (16%)
  local copies, waits for them, and re-layouts  1.04 us (2%)
  between operations  0.77 us (2%)
    ppermute x13, starting transfers between devices, swap(): return lax.ppermute(values, axis, list(enumerate(partner)))  12.5 us
    ppermute x4, starting transfers between devices, doubled(): return added(values, lax.ppermute(values, axis, pairs))  9.63 us
    ppermute x4, waiting for transfers between devices, doubled(): return added(values, lax.ppermute(values, axis, pairs))  8.85 us
    pallas_call x13, Pallas kernels, local_call(): pl.pallas_call(kernel, out_shape=shapes, in_specs=places, out_specs=[pl.B...  7.58 us
    ppermute x13, waiting for transfers between devices, swap(): return lax.ppermute(values, axis, list(enumerate(partner)))  6.21 us
    unnamed x2, local copies, waits for them, and re-layouts  1.04 us
  transfers between devices with their start and end apart: 20, of which 10 were waited for; matrix products, arithmetic and copies ran while one was open for 0% of the time, Pallas kernels for 6%

profile of v1, /device:TPU:0, one launch (start us, length us, event | category | flops | bytes accessed | tf_op | source)
XLA Modules:
  0.0 46.9 jit_solution(17293995395391495357)
XLA Ops:
  0.7 1.0 %copy-done = f32[2,2,128,256]{3,2,1,0:T(8,128)S(1)} copy-done((f32[2,2,128,256]{3,2,1,0:T(8,128)S(1)}, f32[2,2,128,256]{3,2,1,0:T(8,128)}, u32[]{:S(2)}) %copy-start) | copy-done | bytes 524312
  1.7 0.1 shard_map.78
  1.8 3.4 %collective-permute-start = (f32[8,64,128]{2,1,0:T(8,128)S(1)}, f32[8,64,128]{2,1,0:T(8,128)S(1)}, u32[]{:S(2)}, u32[]{:S(2)}) collective-permute-start(f32[8,64,128]{2,1,0:T(8,128)S(1)} %get-tuple-element.31), channel_id=1, source_target_pairs={{0,28},{4,8},{8,4},{12,16},{16,12},{20,24},{24,20},{28,0},{1,29},{... | collective-permute-start | bytes 786440 | tf_op jit(solution)/shard_map/ppermute | solution.py:428
  5.2 1.6 %collective-permute-start.4 = (f32[2,128,128]{2,1,0:T(8,128)S(1)}, f32[2,128,128]{2,1,0:T(8,128)S(1)}, u32[]{:S(2)}, u32[]{:S(2)}) collective-permute-start(f32[2,128,128]{2,1,0:T(8,128)S(1)} %get-tuple-element.35), channel_id=1, source_target_pairs={{0,1},{1,0},{2,3},{3,2},{4,5},{5,4},{6,7},{7,6},{8,9},{9,8},{10,11... | collective-permute-start | bytes 393224 | tf_op jit(solution)/shard_map/ppermute | solution.py:428
  6.8 0.2 collective-permute-start.5
  7.0 1.7 %shard_map.77 = (f32[4,4,256,128]{3,2,1,0:T(8,128)S(1)}, bf16[8,256,256]{2,1,0:T(8,128)(2,1)S(1)}, f32[2,128,128]{2,1,0:T(8,128)S(1)}, f32[4,128,128]{2,1,0:T(8,128)S(1)}, f32[8,128]{1,0:T(8,128)S(1)}) custom-call(s32[4]{0:T(128)} %row_far.1, s32[4]{0:T(128)} %col_far.1, f32[2,2,128,256]{3,2,1,0:T(8,128)} %objects.1, ...), custom_call_target="tpu_custom_call" | custom-call | bytes 4194304 | tf_op jit(solution)/shard_map/pallas_call | solution.py:403
  8.7 2.5 %collective-permute-done.rows.row_cross = f32[8,64,128]{2,1,0:T(8,128)S(1)} collective-permute-done((f32[8,64,128]{2,1,0:T(8,128)S(1)}, f32[8,64,128]{2,1,0:T(8,128)S(1)}, u32[]{:S(2)}, u32[]{:S(2)}) %collective-permute-start) | collective-permute-done | bytes 262176 | tf_op jit(solution)/shard_map/ppermute | solution.py:428
  11.3 0.1 shard_map.79
  11.4 3.1 %collective-permute-start.1 = (f32[2,64,128]{2,1,0:T(8,128)S(1)}, f32[2,64,128]{2,1,0:T(8,128)S(1)}, u32[]{:S(2)}, u32[]{:S(2)}) collective-permute-start(f32[2,64,128]{2,1,0:T(8,128)S(1)} %get-tuple-element.32), channel_id=1, source_target_pairs={{0,1},{1,0},{2,3},{3,2},{4,5},{5,4},{6,7},{7,6},{8,9},{9,8},{10,11... | collective-permute-start | bytes 196616 | tf_op jit(solution)/shard_map/ppermute | solution.py:428
  14.5 0.1 shard_map.80
  14.7 0.6 %collective-permute-start.6 = (f32[88,128]{1,0:T(8,128)S(1)}, f32[88,128]{1,0:T(8,128)S(1)}, u32[]{:S(2)}, u32[]{:S(2)}) collective-permute-start(f32[88,128]{1,0:T(8,128)S(1)} %get-tuple-element.38), channel_id=1, source_target_pairs={{0,4},{4,0},{8,12},{12,8},{16,20},{20,16},{24,28},{28,24},{1,5},{5... | collective-permute-start | bytes 135176 | tf_op jit(solution)/shard_map/ppermute | solution.py:428
  15.2 0.1 collective-permute-start.7
  15.3 0.4 collective-permute-start.8
  15.7 0.9 %collective-permute-done.8.inner_2 = f32[80,128]{1,0:T(8,128)S(1)} collective-permute-done((f32[80,128]{1,0:T(8,128)S(1)}, f32[80,128]{1,0:T(8,128)S(1)}, u32[]{:S(2)}, u32[]{:S(2)}) %collective-permute-start.8) | collective-permute-done | bytes 40992 | tf_op jit(solution)/shard_map/ppermute | solution.py:428
  16.6 0.1 collective-permute-done.1.corner_mate
  16.7 3.8 %shard_map.81 = (f32[4,4,256,128]{3,2,1,0:T(8,128)S(1)}, f32[2,2,128,256]{3,2,1,0:T(8,128)S(1)}, f32[8,64,128]{2,1,0:T(8,128)S(1)}, f32[4,64,128]{2,1,0:T(8,128)...) custom-call(s32[1]{0:T(128)} %bitcast.row_place, ...), custom_call_target="tpu_custom_call", output_to_operand_aliasing={{0}: (11, {})} | custom-call | flops 1610612736 | bytes 8388608 | tf_op jit(solution)/shard_map/pallas_call | solution.py:403
  20.6 0.3 collective-permute-start.10
  20.9 0.2 collective-permute-start.14
  21.2 1.3 %collective-permute-done.14.right = f32[128,128]{1,0:T(8,128)S(1)} collective-permute-done((f32[128,128]{1,0:T(8,128)S(1)}, f32[128,128]{1,0:T(8,128)S(1)}, u32[]{:S(2)}, u32[]{:S(2)}) %collective-permute-start.14) | collective-permute-done | bytes 65568 | tf_op jit(solution)/shard_map/ppermute | solution.py:428
  22.5 0.9 %collective-permute-start.15 = (f32[128,128]{1,0:T(8,128)S(1)}, f32[128,128]{1,0:T(8,128)S(1)}, u32[]{:S(2)}, u32[]{:S(2)}) collective-permute-start(f32[128,128]{1,0:T(8,128)S(1)} %shard_map.84.left), channel_id=1, source_target_pairs={{0,8},{4,12},{8,0},{12,4},{16,24},{20,28},{24,16},{28,20},{1,9},{5... | collective-permute-start | bytes 196616 | tf_op jit(solution)/shard_map/ppermute | solution.py:445
  23.4 3.4 %collective-permute-done.15.right = f32[128,128]{1,0:T(8,128)S(1)} collective-permute-done((f32[128,128]{1,0:T(8,128)S(1)}, f32[128,128]{1,0:T(8,128)S(1)}, u32[]{:S(2)}, u32[]{:S(2)}) %collective-permute-start.15) | collective-permute-done | bytes 65568 | tf_op jit(solution)/shard_map/ppermute | solution.py:445
  26.8 1.2 %collective-permute-start.16 = (f32[128,128]{1,0:T(8,128)S(1)}, f32[128,128]{1,0:T(8,128)S(1)}, u32[]{:S(2)}, u32[]{:S(2)}) collective-permute-start(f32[128,128]{1,0:T(8,128)S(1)} %shard_map.85.left), channel_id=1, source_target_pairs={{0,16},{4,20},{8,24},{12,28},{16,0},{20,4},{24,8},{28,12},{1,17},{... | collective-permute-start | bytes 196616 | tf_op jit(solution)/shard_map/ppermute | solution.py:445
  28.1 2.6 %collective-permute-start.9 = (f32[8,64,128]{2,1,0:T(8,128)S(1)}, f32[8,64,128]{2,1,0:T(8,128)S(1)}, u32[]{:S(2)}, u32[]{:S(2)}) collective-permute-start(f32[8,64,128]{2,1,0:T(8,128)S(1)} %get-tuple-element.43), channel_id=1, source_target_pairs={{0,28},{4,8},{8,4},{12,16},{16,12},{20,24},{24,20},{28,0},{1,29},{... | collective-permute-start | bytes 786440 | tf_op jit(solution)/shard_map/ppermute | solution.py:428
  30.7 0.4 collective-permute-done.16.right
  31.2 3.2 %collective-permute-start.17 = (f32[128,128]{1,0:T(8,128)S(1)}, f32[128,128]{1,0:T(8,128)S(1)}, u32[]{:S(2)}, u32[]{:S(2)}) collective-permute-start(f32[128,128]{1,0:T(8,128)S(1)} %shard_map.86.left), channel_id=1, source_target_pairs={{0,1},{1,0},{2,3},{3,2},{4,5},{5,4},{6,7},{7,6},{8,9},{9,8},{10,11... | collective-permute-start | bytes 196616 | tf_op jit(solution)/shard_map/ppermute | solution.py:445
  34.4 2.2 %collective-permute-done.17.right = f32[128,128]{1,0:T(8,128)S(1)} collective-permute-done((f32[128,128]{1,0:T(8,128)S(1)}, f32[128,128]{1,0:T(8,128)S(1)}, u32[]{:S(2)}, u32[]{:S(2)}) %collective-permute-start.17) | collective-permute-done | bytes 65568 | tf_op jit(solution)/shard_map/ppermute | solution.py:445
  36.6 4.3 %collective-permute-start.18 = (f32[128,128]{1,0:T(8,128)S(1)}, f32[128,128]{1,0:T(8,128)S(1)}, u32[]{:S(2)}, u32[]{:S(2)}) collective-permute-start(f32[128,128]{1,0:T(8,128)S(1)} %shard_map.87.left), channel_id=1, source_target_pairs={{0,2},{1,3},{2,0},{3,1},{4,6},{5,7},{6,4},{7,5},{8,10},{9,11},{10,... | collective-permute-start | bytes 196616 | tf_op jit(solution)/shard_map/ppermute | solution.py:445
  41.1 2.7 %collective-permute-done.18.right = f32[128,128]{1,0:T(8,128)S(1)} collective-permute-done((f32[128,128]{1,0:T(8,128)S(1)}, f32[128,128]{1,0:T(8,128)S(1)}, u32[]{:S(2)}, u32[]{:S(2)}) %collective-permute-start.18) | collective-permute-done | bytes 65568 | tf_op jit(solution)/shard_map/ppermute | solution.py:445
  43.9 1.2 %collective-permute-done.19.probe_other = f32[128,128]{1,0:T(8,128)S(1)} collective-permute-done((f32[128,128]{1,0:T(8,128)S(1)}, f32[128,128]{1,0:T(8,128)S(1)}, u32[]{:S(2)}, u32[]{:S(2)}) %collective-permute-start.19) | collective-permute-done | bytes 65568 | tf_op jit(solution)/shard_map/ppermute | solution.py:428
  45.2 0.7 %shard_map.89 = f32[2,128,128]{2,1,0:T(8,128)} custom-call(s32[1]{0:T(128)} %bitcast.row_place, f32[128,128]{1,0:T(8,128)S(1)} %shard_map.88.probe_half, f32[128,128]{1,0:T(8,128)S(1)} %collective-permute-done.19.probe_other), custom_call_target="tpu_custom_call" | custom-call | bytes 1048576 | tf_op jit(solution)/shard_map/pallas_call | solution.py:403
  45.8 0.1 collective-permute-done.12.col_mate
  46.0 1.0 %shard_map.83 = f32[2,2,128,256]{3,2,1,0:T(8,128)} custom-call(s32[1]{0:T(128)} %bitcast.row_place, s32[1]{0:T(128)} %bitcast.1.col_place, f32[2,2,128,256]{3,2,1,0:T(8,128)S(1)} %get-tuple-element.42.own, f32[8,64,128]{2,1,0:T(8,128)S(1)} %collective-permute-done.9.row_cross, f32[12,64,128]{2,1,0:T(8,128)S(1)} %collective-permute-done.10.row_mate, ...), custom_call_target="tpu_custom_call" | custom-call | bytes 1048576 | tf_op jit(solution)/shard_map/pallas_call | solution.py:403
  (23 shorter events, 0.3 us)
Async XLA Ops:
  0.7 1.0 %copy-start = (f32[2,2,128,256]{3,2,1,0:T(8,128)S(1)}, f32[2,2,128,256]{3,2,1,0:T(8,128)}, u32[]{:S(2)}) copy-start(f32[2,2,128,256]{3,2,1,0:T(8,128)} %objects.1) | copy-start | bytes 1572868
  1.8 9.4 %collective-permute-start = (f32[8,64,128]{2,1,0:T(8,128)S(1)}, f32[8,64,128]{2,1,0:T(8,128)S(1)}, u32[]{:S(2)}, u32[]{:S(2)}) collective-permute-start(f32[8,64,128]{2,1,0:T(8,128)S(1)} %get-tuple-element.31), channel_id=1, source_target_pairs={{0,28},{4,8},{8,4},{12,16},{16,12},{20,24},{24,20},{28,0},{1,29},{... | collective-permute-start | bytes 786440 | tf_op jit(solution)/shard_map/ppermute | solution.py:428
  5.2 9.3 %collective-permute-start.3 = (f32[8,64,128]{2,1,0:T(8,128)S(1)}, f32[8,64,128]{2,1,0:T(8,128)S(1)}, u32[]{:S(2)}, u32[]{:S(2)}) collective-permute-start(f32[8,64,128]{2,1,0:T(8,128)S(1)} %get-tuple-element.34), channel_id=1, source_target_pairs={{0,4},{4,0},{8,12},{12,8},{16,20},{20,16},{24,28},{28,24},{1,5},{5... | collective-permute-start | bytes 786440 | tf_op jit(solution)/shard_map/ppermute | solution.py:428
  5.2 9.3 %collective-permute-start.4 = (f32[2,128,128]{2,1,0:T(8,128)S(1)}, f32[2,128,128]{2,1,0:T(8,128)S(1)}, u32[]{:S(2)}, u32[]{:S(2)}) collective-permute-start(f32[2,128,128]{2,1,0:T(8,128)S(1)} %get-tuple-element.35), channel_id=1, source_target_pairs={{0,1},{1,0},{2,3},{3,2},{4,5},{5,4},{6,7},{7,6},{8,9},{9,8},{10,11... | collective-permute-start | bytes 393224 | tf_op jit(solution)/shard_map/ppermute | solution.py:428
  6.8 7.7 %collective-permute-start.5 = (f32[2,128,128]{2,1,0:T(8,128)S(1)}, f32[2,128,128]{2,1,0:T(8,128)S(1)}, u32[]{:S(2)}, u32[]{:S(2)}) collective-permute-start(f32[2,128,128]{2,1,0:T(8,128)S(1)} %get-tuple-element.36), channel_id=1, source_target_pairs={{0,4},{1,2},{2,1},{3,7},{4,0},{5,6},{6,5},{7,3},{8,12},{9,10},{10,... | collective-permute-start | bytes 393224 | tf_op jit(solution)/shard_map/ppermute | solution.py:440
  11.4 5.4 %collective-permute-start.1 = (f32[2,64,128]{2,1,0:T(8,128)S(1)}, f32[2,64,128]{2,1,0:T(8,128)S(1)}, u32[]{:S(2)}, u32[]{:S(2)}) collective-permute-start(f32[2,64,128]{2,1,0:T(8,128)S(1)} %get-tuple-element.32), channel_id=1, source_target_pairs={{0,1},{1,0},{2,3},{3,2},{4,5},{5,4},{6,7},{7,6},{8,9},{9,8},{10,11... | collective-permute-start | bytes 196616 | tf_op jit(solution)/shard_map/ppermute | solution.py:428
  14.5 2.2 %collective-permute-start.2 = (f32[2,64,128]{2,1,0:T(8,128)S(1)}, f32[2,64,128]{2,1,0:T(8,128)S(1)}, u32[]{:S(2)}, u32[]{:S(2)}) collective-permute-start(f32[2,64,128]{2,1,0:T(8,128)S(1)} %get-tuple-element.33), channel_id=1, source_target_pairs={{0,4},{1,2},{2,1},{3,7},{4,0},{5,6},{6,5},{7,3},{8,12},{9,10},{10,... | collective-permute-start | bytes 196616 | tf_op jit(solution)/shard_map/ppermute | solution.py:440
  14.7 2.0 %collective-permute-start.6 = (f32[88,128]{1,0:T(8,128)S(1)}, f32[88,128]{1,0:T(8,128)S(1)}, u32[]{:S(2)}, u32[]{:S(2)}) collective-permute-start(f32[88,128]{1,0:T(8,128)S(1)} %get-tuple-element.38), channel_id=1, source_target_pairs={{0,4},{4,0},{8,12},{12,8},{16,20},{20,16},{24,28},{28,24},{1,5},{5... | collective-permute-start | bytes 135176 | tf_op jit(solution)/shard_map/ppermute | solution.py:428
  15.2 1.4 %collective-permute-start.7 = (f32[88,128]{1,0:T(8,128)S(1)}, f32[88,128]{1,0:T(8,128)S(1)}, u32[]{:S(2)}, u32[]{:S(2)}) collective-permute-start(f32[88,128]{1,0:T(8,128)S(1)} %get-tuple-element.39), channel_id=1, source_target_pairs={{0,4},{4,0},{8,12},{12,8},{16,20},{20,16},{24,28},{28,24},{1,5},{5... | collective-permute-start | bytes 135176 | tf_op jit(solution)/shard_map/ppermute | solution.py:428
  15.3 1.3 %collective-permute-start.8 = (f32[80,128]{1,0:T(8,128)S(1)}, f32[80,128]{1,0:T(8,128)S(1)}, u32[]{:S(2)}, u32[]{:S(2)}) collective-permute-start(f32[80,128]{1,0:T(8,128)S(1)} %get-tuple-element.40), channel_id=1, source_target_pairs={{0,4},{4,0},{8,12},{12,8},{16,20},{20,16},{24,28},{28,24},{1,5},{5... | collective-permute-start | bytes 122888 | tf_op jit(solution)/shard_map/ppermute | solution.py:428
  20.6 20.3 %collective-permute-start.10 = (f32[12,64,128]{2,1,0:T(8,128)S(1)}, f32[12,64,128]{2,1,0:T(8,128)S(1)}, u32[]{:S(2)}, u32[]{:S(2)}) collective-permute-start(f32[12,64,128]{2,1,0:T(8,128)S(1)} %get-tuple-element.44), channel_id=1, source_target_pairs={{0,4},{4,0},{8,12},{12,8},{16,20},{20,16},{24,28},{28,24},{1,5},{5... | collective-permute-start | bytes 1179656 | tf_op jit(solution)/shard_map/ppermute | solution.py:428
  20.9 1.6 %collective-permute-start.14 = (f32[128,128]{1,0:T(8,128)S(1)}, f32[128,128]{1,0:T(8,128)S(1)}, u32[]{:S(2)}, u32[]{:S(2)}) collective-permute-start(f32[128,128]{1,0:T(8,128)S(1)} %get-tuple-element.51), channel_id=1, source_target_pairs={{0,4},{4,0},{8,12},{12,8},{16,20},{20,16},{24,28},{28,24},{1,5},{5... | collective-permute-start | bytes 196616 | tf_op jit(solution)/shard_map/ppermute | solution.py:428
  22.5 4.3 %collective-permute-start.15 = (f32[128,128]{1,0:T(8,128)S(1)}, f32[128,128]{1,0:T(8,128)S(1)}, u32[]{:S(2)}, u32[]{:S(2)}) collective-permute-start(f32[128,128]{1,0:T(8,128)S(1)} %shard_map.84.left), channel_id=1, source_target_pairs={{0,8},{4,12},{8,0},{12,4},{16,24},{20,28},{24,16},{28,20},{1,9},{5... | collective-permute-start | bytes 196616 | tf_op jit(solution)/shard_map/ppermute | solution.py:445
  26.8 4.3 %collective-permute-start.16 = (f32[128,128]{1,0:T(8,128)S(1)}, f32[128,128]{1,0:T(8,128)S(1)}, u32[]{:S(2)}, u32[]{:S(2)}) collective-permute-start(f32[128,128]{1,0:T(8,128)S(1)} %shard_map.85.left), channel_id=1, source_target_pairs={{0,16},{4,20},{8,24},{12,28},{16,0},{20,4},{24,8},{28,12},{1,17},{... | collective-permute-start | bytes 196616 | tf_op jit(solution)/shard_map/ppermute | solution.py:445
  28.1 12.8 %collective-permute-start.11 = (f32[4,64,128]{2,1,0:T(8,128)S(1)}, f32[4,64,128]{2,1,0:T(8,128)S(1)}, u32[]{:S(2)}, u32[]{:S(2)}) collective-permute-start(f32[4,64,128]{2,1,0:T(8,128)S(1)} %get-tuple-element.47), channel_id=1, source_target_pairs={{0,28},{4,8},{8,4},{12,16},{16,12},{20,24},{24,20},{28,0},{1,29},{... | collective-permute-start | bytes 393224 | tf_op jit(solution)/shard_map/ppermute | solution.py:428
  28.1 17.8 %collective-permute-start.9 = (f32[8,64,128]{2,1,0:T(8,128)S(1)}, f32[8,64,128]{2,1,0:T(8,128)S(1)}, u32[]{:S(2)}, u32[]{:S(2)}) collective-permute-start(f32[8,64,128]{2,1,0:T(8,128)S(1)} %get-tuple-element.43), channel_id=1, source_target_pairs={{0,28},{4,8},{8,4},{12,16},{16,12},{20,24},{24,20},{28,0},{1,29},{... | collective-permute-start | bytes 786440 | tf_op jit(solution)/shard_map/ppermute | solution.py:428
  31.2 5.5 %collective-permute-start.17 = (f32[128,128]{1,0:T(8,128)S(1)}, f32[128,128]{1,0:T(8,128)S(1)}, u32[]{:S(2)}, u32[]{:S(2)}) collective-permute-start(f32[128,128]{1,0:T(8,128)S(1)} %shard_map.86.left), channel_id=1, source_target_pairs={{0,1},{1,0},{2,3},{3,2},{4,5},{5,4},{6,7},{7,6},{8,9},{9,8},{10,11... | collective-permute-start | bytes 196616 | tf_op jit(solution)/shard_map/ppermute | solution.py:445
  36.6 7.2 %collective-permute-start.18 = (f32[128,128]{1,0:T(8,128)S(1)}, f32[128,128]{1,0:T(8,128)S(1)}, u32[]{:S(2)}, u32[]{:S(2)}) collective-permute-start(f32[128,128]{1,0:T(8,128)S(1)} %shard_map.87.left), channel_id=1, source_target_pairs={{0,2},{1,3},{2,0},{3,1},{4,6},{5,7},{6,4},{7,5},{8,10},{9,11},{10,... | collective-permute-start | bytes 196616 | tf_op jit(solution)/shard_map/ppermute | solution.py:445
  40.9 5.0 %collective-permute-start.12 = (f32[2,128,128]{2,1,0:T(8,128)S(1)}, f32[2,128,128]{2,1,0:T(8,128)S(1)}, u32[]{:S(2)}, u32[]{:S(2)}) collective-permute-start(f32[2,128,128]{2,1,0:T(8,128)S(1)} %get-tuple-element.48), channel_id=1, source_target_pairs={{0,1},{1,0},{2,3},{3,2},{4,5},{5,4},{6,7},{7,6},{8,9},{9,8},{10,11... | collective-permute-start | bytes 393224 | tf_op jit(solution)/shard_map/ppermute | solution.py:428
  41.0 5.0 %collective-permute-start.13 = (f32[2,128,128]{2,1,0:T(8,128)S(1)}, f32[2,128,128]{2,1,0:T(8,128)S(1)}, u32[]{:S(2)}, u32[]{:S(2)}) collective-permute-start(f32[2,128,128]{2,1,0:T(8,128)S(1)} %get-tuple-element.49), channel_id=1, source_target_pairs={{0,4},{1,2},{2,1},{3,7},{4,0},{5,6},{6,5},{7,3},{8,12},{9,10},{10,... | collective-permute-start | bytes 393224 | tf_op jit(solution)/shard_map/ppermute | solution.py:440
  43.8 1.3 %collective-permute-start.19 = (f32[128,128]{1,0:T(8,128)S(1)}, f32[128,128]{1,0:T(8,128)S(1)}, u32[]{:S(2)}, u32[]{:S(2)}) collective-permute-start(f32[128,128]{1,0:T(8,128)S(1)} %shard_map.88.probe_half), channel_id=1, source_target_pairs={{0,4},{4,0},{8,12},{12,8},{16,20},{20,16},{24,28},{28,24},{1,5},{5... | collective-permute-start | bytes 196616 | tf_op jit(solution)/shard_map/ppermute | solution.py:428
